TPU v7x, 256 devices: a whole 4x4x8 slice. The times are simulated.
256 devices in a mesh: row: 8 (over x, core), col: 32 (over z, y).
Axes of the slice: x: 4, y: 4, z: 8, core: 2. Of those that a mesh axis runs over, the one named last changes fastest.
Arguments:
- images: bfloat16 [24576, 768], P(('row', 'col')), may hold values from -16 to 16
- texts: bfloat16 [24576, 768], P(('row', 'col')), may hold values from -16 to 16
- logit_scale: float32 [1], replicated, may hold values from 0.05 to 0.15
Outputs:
- loss: float32 [1], replicated
- grad_images: float32 [24576, 768], P(('row', 'col'))
- grad_texts: float32 [24576, 768], P(('row', 'col'))
All inputs are finite; a program needn't handle non-finite values.
Results may differ from a plain program's by a relative error of at most 0.002.
Values may be sent and summed in bfloat16 or wider, within the bound.
A program may use at most 192 MiB of HBM per device.

v0:
```python
import functools
import math

import jax
import jax.numpy as jnp
from jax import lax
from jax.experimental import pallas as pl
from jax.experimental.pallas import tpu as pltpu
from jax.sharding import PartitionSpec as P

MESH = pl.DeviceIdType.MESH
F32 = jnp.float32
BF16 = jnp.bfloat16
NT = (((1,), (1,)), ((), ()))
NN = (((1,), (0,)), ((), ()))
TN = (((0,), (0,)), ((), ()))
LN2 = math.log(2.0)
NX, NY, NZ, NC = 4, 4, 8, 2
R = 96
HALF = R // 2
PIECES = 3
PIECE = R // PIECES
E = 768
SLOTS = 16
B = SLOTS * R
LANES = 128
GROUPS = B // LANES
TILE = 4 * R
CHUNK = 256

ZSTEPS = [0, 7, 2, 6, 1, 3, 5, 4]
ZPLACE = [ZSTEPS.index(d) for d in range(NZ)]
USTEPS = [0, 1, 3, 2]
UPLACE = [USTEPS.index(d) for d in range(4)]


def tree(f, parts):
    parts = list(parts)
    while len(parts) > 1:
        parts = [f(*parts[k:k + 2]) if k + 1 < len(parts) else parts[k] for k in range(0, len(parts), 2)]
    return parts[0]


def copy(src, dst, send, recv, to):
    return pltpu.make_async_remote_copy(
        src_ref=src, dst_ref=dst, send_sem=send, recv_sem=recv, device_id=to, device_id_type=MESH
    )


def rows_of(slot, count=R):
    return pl.ds(slot * R, count)


def lse_first(top, total=None):
    high = jnp.max(top, axis=0, keepdims=True)
    part = jnp.exp2(top - high)
    part = part if total is None else part * total
    return high + jnp.log2(jnp.sum(part, axis=0, keepdims=True))


def kernel(
    images, texts, scale_ref, loss_out, gi_out, gt_out,
    ibuf, tbuf, scores, weights, row_top, row_sum, col_part, col_shift,
    row_lse, row_shift, st_c, st_z, st_t, all_i, all_t, ls_c, ls_z, ls_x, ls_y,
    p_sib, p_in, p_own, p_send, p_recv, f_recv, h_recv, q_send, q_recv, q_own, r_recv,
    zi_s, zi_r, fi_s, fi_r, ti_s, ti_r, sc_s, sc_r, sz_s, sz_r, st_s, st_r,
    lc_s, lc_r, lz_s, lz_r, lx_s, lx_r, ly_s, ly_r, ps_s, ps_r, pz_s, pz_r, q_s, q_r, r_s, r_r,
):
    row, col = lax.axis_index("row"), lax.axis_index("col")
    x, c, z, y = row // NC, lax.rem(row, NC), col // NY, lax.rem(col, NY)
    u, v = x * (1 - c) + y * c, y * (1 - c) + x * c
    scale = scale_ref[0]

    def to(dx=0, dy=0, dz=0, dc=0):
        return (lax.rem(x + dx, NX) * NC + lax.rem(c + dc, NC), lax.rem(z + dz, NZ) * NY + lax.rem(y + dy, NY))

    def to_uv(du=0, dv=0):
        return to(dx=du * (1 - c) + dv * c, dy=dv * (1 - c) + du * c)

    sib = to(dc=1)
    started = []

    def launch(cp):
        cp.start()
        started.append(cp)
        return cp

    barrier = pltpu.get_barrier_semaphore()
    uv_steps = [(du, dv) for du in USTEPS for dv in USTEPS if (du, dv) != (0, 0)]
    partners = [sib] + [to(dz=d) for d in ZSTEPS[1:]] + [to(dx=du, dy=dv) for du, dv in uv_steps]
    for d in partners:
        pl.semaphore_signal(barrier, inc=1, device_id=d, device_id_type=MESH)
    pl.semaphore_wait(barrier, len(partners))

    def z_copy(s, hop, i):
        k = (0 if s == 1 else 12) + (hop - 1) * PIECES + i
        src = pl.ds(ZPLACE[(-s * (hop - 1)) % NZ] * R + i * PIECE, PIECE)
        dst = pl.ds(ZPLACE[(-s * hop) % NZ] * R + i * PIECE, PIECE)
        held = images.at[pl.ds(i * PIECE, PIECE)] if hop == 1 else ibuf.at[src]
        return copy(held, ibuf.at[dst], zi_s.at[k], zi_r.at[k], to(dz=s % NZ))

    def last_hop(s):
        return (0, 1) if s == 1 else (2,)

    def z_arrive(s, hop):
        for i in last_hop(s) if hop == 4 else range(PIECES):
            z_copy(s, hop, i).wait_recv()
            if hop < 3 or (hop == 3 and i in last_hop(s)):
                launch(z_copy(s, hop + 1, i))
        if hop < 4:
            forward(ZPLACE[(-s * hop) % NZ] * R, R)
        else:
            forward(ZPLACE[4] * R + last_hop(s)[0] * PIECE, PIECE * len(last_hop(s)))

    forwards = []

    def forward(start, count):
        k = len(forwards)
        src = images if start == 0 else ibuf.at[pl.ds(start, count)]
        forwards.append(launch(copy(src, ibuf.at[pl.ds(B // 2 + start, count)], fi_s.at[k], fi_r.at[k], sib)))

    def v_copy(s, hop):
        k = 2 if hop == 2 else (0 if s == 1 else 1)
        dst = rows_of(UPLACE[(-s * hop) % 4])
        return copy(texts, tbuf.at[dst], ti_s.at[k], ti_r.at[k], to_uv(dv=s * hop % 4))

    def u_copy(s, hop, pv):
        src, dst = 4 * UPLACE[(-s * (hop - 1)) % 4] + pv, 4 * UPLACE[(-s * hop) % 4] + pv
        k = 3 + pv * 3 + (2 if hop == 2 else (0 if s == 1 else 1))
        held = texts if hop == 1 and pv == 0 else tbuf.at[rows_of(src)]
        return copy(held, tbuf.at[rows_of(dst)], ti_s.at[k], ti_r.at[k], to_uv(du=s % 4))

    def v_arrive(s, hop):
        v_copy(s, hop).wait_recv()
        pv = UPLACE[(-s * hop) % 4]
        launch(u_copy(1, 1, pv))
        launch(u_copy(-1, 1, pv))

    def u_arrive(s, hop, pv):
        u_copy(s, hop, pv).wait_recv()
        if hop == 1 and s == (1 if pv % 2 == 0 else -1):
            launch(u_copy(s, 2, pv))

    for i in range(PIECES):
        launch(z_copy(1, 1, i))
        launch(z_copy(-1, 1, i))
        if i == 0:
            launch(v_copy(1, 1))
            launch(v_copy(-1, 1))
    launch(v_copy(1, 2))
    launch(u_copy(1, 1, 0))
    launch(u_copy(-1, 1, 0))
    forward(0, R)
    ibuf[rows_of(0)] = images[...]
    tbuf[rows_of(0)] = texts[...]
    matched = images[...].astype(F32) * texts[...].astype(F32)
    matched = jnp.sum(matched, axis=0, keepdims=True)
    matched = tree(jnp.add, [matched[:, g:g + LANES - R] for g in range(0, E, LANES - R)])
    z_arrive(1, 1)
    z_arrive(-1, 1)
    v_arrive(1, 1)
    v_arrive(-1, 1)
    u_arrive(1, 1, 0)
    u_arrive(-1, 1, 0)
    z_arrive(1, 2)
    z_arrive(-1, 2)
    v_arrive(1, 2)
    for pv in (2, 1):
        u_arrive(1, 1, pv)
        u_arrive(-1, 1, pv)
    z_arrive(1, 3)
    z_arrive(-1, 3)
    u_arrive(1, 1, 3)
    u_arrive(-1, 1, 3)
    for cp in forwards:
        cp.wait_recv()

    scale2 = scale * (1.0 / LN2)
    late = 7 * R
    early_n = 12 * R

    def score_block(r0, part, count, c0, width, merge, lse_slot):
        rows = pl.ds(r0, count)
        tile = scale2 * lax.dot_general(ibuf[rows, :], tbuf[pl.ds(c0, width), :], NT, preferred_element_type=F32)
        scores[rows, pl.ds(c0, width)] = tile
        for r in range(0, count, 32):
            sub = pl.ds(r0 + r, 32)
            parts = [tile[r:r + 32, g:g + LANES] for g in range(0, width, LANES)]
            top = tree(jnp.maximum, parts)
            if merge:
                old = row_top[sub, :]
                top = jnp.maximum(top, old)
            total = tree(jnp.add, [jnp.exp2(w - top) for w in parts])
            if merge:
                total = total + row_sum[sub, :] * jnp.exp2(old - top)
            row_top[sub, :] = top
            row_sum[sub, :] = total
        if lse_slot is not None:
            lse = lse_first(row_top[rows, :].T, row_sum[rows, :].T)
            row_lse[lse_slot, :, 0:count] = jnp.broadcast_to(lse, (8, count))
        for g in range(0, width, LANES):
            parts = [tile[r:r + 8, g:g + LANES] for r in range(0, count, 8)]
            top = tree(jnp.maximum, parts)
            col_part[0, part, c0 + g:c0 + g + LANES] = top
            col_part[1, part, c0 + g:c0 + g + LANES] = tree(jnp.add, [jnp.exp2(w - top) for w in parts])

    def eight(t):
        return pl.ds(pl.multiple_of(t * 8, 8), 8)

    def early_row(t):
        return pl.multiple_of((t // 3) * (B // 2) + lax.rem(t, 3) * (late // 3), 32)

    @pl.loop(0, 6, unroll=6)
    def _(t):
        score_block(early_row(t), eight(t), late // 3, 0, early_n, False, None)

    waiting = len(forwards)
    z_arrive(1, 4)
    z_arrive(-1, 4)
    for pv in range(4):
        u_arrive(1 if pv % 2 == 0 else -1, 2, pv)

    @pl.loop(0, 6, unroll=6)
    def _(t):
        score_block(early_row(t), eight(t), late // 3, early_n, B - early_n, True, t)

    for cp in forwards[waiting:]:
        cp.wait_recv()

    @pl.loop(6, 8, unroll=2)
    def _(t):
        score_block(pl.multiple_of((t - 6) * (B // 2) + late, 32), eight(t), R, 0, B, False, t)

    me_t = u * 4 + v

    def i_row(k):
        return lax.rem(c + k // NZ, NC) * NZ + lax.rem(z + ZSTEPS[k % NZ], NZ)

    def t_row(k):
        return lax.rem(u + USTEPS[k // 4], 4) * 4 + lax.rem(v + USTEPS[k % 4], 4)

    def spread(st, mine, steps, where, ss, rs):
        return [launch(copy(st.at[mine], st.at[mine], ss.at[k], rs.at[k], where(d))) for k, d in enumerate(steps)]

    def along_z(d):
        return to(dz=d)

    st_c[c] = jnp.full((SLOTS, LANES), -1e30, F32)
    st_c[c, pl.ds(c * NZ + z, 1), R:LANES] = matched
    lse = []
    for core in range(2):
        lse += [row_lse[t, 0:1, 0:late // 3] for t in range(core * 3, core * 3 + 3)] + [row_lse[6 + core, 0:1, 0:R]]
    lse = jnp.concatenate(lse, axis=1)
    for k in range(SLOTS):
        st_c[c, pl.ds(i_row(k), 1), 0:R] = lse[:, k * R:(k + 1) * R]
    c_cp = launch(copy(st_c.at[c], st_c.at[c], sc_s.at[0], sc_r.at[0], sib))
    st_t[me_t] = jnp.zeros((SLOTS, LANES), F32)
    lse = lse_first(col_part[0], col_part[1])
    for k in range(SLOTS):
        st_t[me_t, pl.ds(t_row(k), 1), 0:R] = lse[:, k * R:(k + 1) * R]
    t_cps = spread(st_t, me_t, uv_steps, lambda d: to_uv(*d), st_s, st_r)
    c_cp.wait_recv()
    st_z[z] = lse_first(st_c[...])[0]
    z_cps = spread(st_z, z, ZSTEPS[1:], along_z, sz_s, sz_r)
    half = jnp.log2(jnp.full((1, LANES), scale * 0.5, F32))
    for cp in t_cps:
        cp.wait_recv()
    all_t[...] = lse_first(st_t[...])[0]
    for k in range(SLOTS):
        col_shift[0:1, k * R:(k + 1) * R] = (all_t[pl.ds(t_row(k), 1), :] - half)[:, 0:R]
    for cp in z_cps:
        cp.wait_recv()
    all_i[...] = lse_first(st_z[...])[0]
    for k in range(SLOTS):
        row_shift[k:k + 1, :] = all_i[pl.ds(i_row(k), 1), :] - half

    lane = lax.broadcasted_iota(jnp.int32, (1, LANES), 1)
    sum_i = jnp.sum(all_i[...], axis=0, keepdims=True) * jnp.where(lane < R, LN2, -2.0 * scale)
    sum_t = jnp.where(lane < R, LN2 * jnp.sum(all_t[...], axis=0, keepdims=True), 0.0)

    def total_of(st, n):
        return functools.reduce(jnp.add, [st[k] for k in range(n)])

    ls_x[x] = jnp.broadcast_to(sum_i, (8, LANES))
    ls_c[c] = jnp.broadcast_to(sum_t, (8, LANES))
    lx_cps = spread(ls_x, x, USTEPS[1:], lambda d: to(dx=d), lx_s, lx_r)
    lc_cps = [launch(copy(ls_c.at[c], ls_c.at[c], lc_s.at[0], lc_r.at[0], sib))]

    def make_weights(slot, c0, width, first=False):
        @pl.loop(slot, slot + 4, unroll=4)
        def _(k):
            rows = pl.ds(pl.multiple_of(k * R, R), R)
            if first:
                shift = jnp.broadcast_to(row_shift[pl.ds(k, 1), :], (LANES, LANES)).T[0:R]
                row_top[rows, :] = shift
            else:
                shift = row_top[rows, :]
            for g in range(c0, c0 + width, LANES):
                cols = pl.ds(g, LANES)
                w = scores[rows, cols]
                w = jnp.exp2(w - shift) + jnp.exp2(w - col_shift[0:1, cols])
                weights[rows, cols] = w.astype(BF16)

    def near_weights(p):
        for slot in (0, 8):
            make_weights(slot, p * TILE, TILE, p == 3)

    def p_tile(slot):
        return lax.dot_general(weights[rows_of(slot, TILE), :], tbuf[...], NN, preferred_element_type=F32)

    def sib_copy(h):
        rows = pl.ds(h * TILE, TILE)
        return copy(p_sib.at[rows], p_in.at[rows], ps_s.at[h], ps_r.at[h], sib)

    def do_sib(h):
        p_sib[pl.ds(h * TILE, TILE)] = p_tile(8 + 4 * h)
        launch(sib_copy(h))

    def p_copy(k):
        if k == 0 or k == 7:
            dz, rows = (2, 0) if k == 0 else (6, HALF)
            src = p_send.at[pl.ds(7 * R + rows, HALF)]
            return copy(src, h_recv.at[rows // HALF], pz_s.at[k], pz_r.at[k], to(dz=dz))
        src = p_send.at[rows_of(k)]
        if k in (5, 6):
            return copy(src, f_recv.at[k - 5], pz_s.at[k], pz_r.at[k], to(dz=1 if k == 5 else 7))
        return copy(src, p_recv.at[k - 1], pz_s.at[k], pz_r.at[k], to(dz=ZSTEPS[k]))

    def own_tile(h):
        tile = p_tile(4 * h)
        sib_copy(h).wait_recv()
        return tile + p_in[pl.ds(h * TILE, TILE)]

    def do_far():
        p_send[pl.ds(TILE, TILE)] = own_tile(1).astype(BF16)
        for k in (5, 6, 0, 7, 4):
            launch(p_copy(k))

    def do_near():
        tile = own_tile(0)
        p_own[...] = tile
        p_send[rows_of(1)] = tile[R:2 * R].astype(BF16)
        launch(p_copy(1))

    def do_merge():
        for k in (5, 0, 6, 7):
            p_copy(k).wait_recv()
        for i in range(2):
            @pl.loop(0, HALF // 16)
            def _(t, i=i):
                near = pl.multiple_of(t * 16, 16)
                for base, with_half in ((i * HALF, True), (HALF - i * HALF, False)):
                    rows = pl.ds(base + near, 16)
                    out = pl.ds((2 + i) * R + base + near, 16)
                    w = p_own[out] + f_recv[i, rows].astype(F32)
                    if with_half:
                        w = w + h_recv[i, pl.ds(near, 16)].astype(F32)
                    p_send[out] = w.astype(BF16)
            launch(p_copy(2 + i))

    def q_copy(p, pv):
        k = (p - 1) * 4 + pv
        return copy(q_send.at[p - 1, rows_of(pv)], q_recv.at[p - 1, rows_of(pv)], q_s.at[k], q_r.at[k], to_uv(du=USTEPS[p]))

    def do_q(p):
        tile = lax.dot_general(weights[:, rows_of(4 * p, TILE)], ibuf[...], TN, preferred_element_type=F32)
        if p:
            q_send[p - 1] = tile.astype(BF16)
            for pv in (3, 1, 2, 0):
                launch(q_copy(p, pv))
        else:
            q_own[...] = tile

    def r_copy(p):
        return copy(q_own.at[rows_of(p)], r_recv.at[p - 1], r_s.at[p - 1], r_r.at[p - 1], to_uv(dv=USTEPS[p]))

    make_weights(12, 0, B, True)
    do_sib(1)
    make_weights(4, 0, B, True)
    near_weights(3)
    do_q(3)
    for cp in lx_cps + lc_cps:
        cp.wait_recv()
    ls_y[y] = total_of(ls_x, NX)
    ls_z[z] = total_of(ls_c, NC)
    ly_cps = spread(ls_y, y, USTEPS[1:], lambda d: to(dy=d), ly_s, ly_r)
    lz_cps = spread(ls_z, z, ZSTEPS[1:], along_z, lz_s, lz_r)
    do_far()
    near_weights(1)
    do_q(1)
    near_weights(2)
    do_q(2)
    near_weights(0)
    do_sib(0)
    do_q(0)
    do_near()
    do_merge()
    for cp in ly_cps + lz_cps:
        cp.wait_recv()
    total = total_of(ls_y, NY) + total_of(ls_z, NZ)
    loss_out[0] = jnp.sum(total[0:1]) * (1.0 / (2.0 * R * NX * NY * NZ * NC))

    for pv in (3, 1, 2, 0):
        for p in range(1, 4):
            q_copy(p, pv).wait_recv()

        @pl.loop(0, R // 32)
        def _(t, pv=pv):
            rows = pl.ds(pl.multiple_of(pv * R + t * 32, 32), 32)
            q_own[rows] = functools.reduce(jnp.add, [q_recv[k, rows].astype(F32) for k in range(3)], q_own[rows])
        if pv:
            launch(r_copy(pv))
    for k in range(1, 5):
        p_copy(k).wait_recv()

    @pl.loop(0, R // 16)
    def _(t):
        rows = pl.ds(pl.multiple_of(t * 16, 16), 16)
        gi = p_own[rows] - scale * texts[rows].astype(F32)
        gi_out[rows] = functools.reduce(jnp.add, [p_recv[k, rows].astype(F32) for k in range(4)], gi)

    for p in range(1, 4):
        r_copy(p).wait_recv()

    @pl.loop(0, R // 16)
    def _(t):
        rows = pl.ds(pl.multiple_of(t * 16, 16), 16)
        gt = q_own[rows] - scale * images[rows].astype(F32)
        gt_out[rows] = functools.reduce(jnp.add, [r_recv[k, rows] for k in range(3)], gt)

    for cp in started:
        cp.wait_send()


def local(images, texts, logit_scale):
    vmem = pl.BlockSpec(memory_space=pltpu.VMEM)
    smem = pl.BlockSpec(memory_space=pltpu.SMEM)
    dma = pltpu.SemaphoreType.DMA
    scratch = [
        pltpu.VMEM((B, E), BF16), pltpu.VMEM((B, E), BF16), pltpu.VMEM((B, B), F32), pltpu.VMEM((B, B), BF16),
        pltpu.VMEM((B, LANES), F32), pltpu.VMEM((B, LANES), F32),
        pltpu.VMEM((2, 64, B), F32), pltpu.VMEM((8, B), F32),
    ]
    scratch += [pltpu.VMEM((8, 8, 2 * LANES), F32), pltpu.VMEM((SLOTS, LANES), F32)]
    scratch += [pltpu.VMEM((n, SLOTS, LANES), F32) for n in (NC, NZ)]
    scratch += [pltpu.VMEM((SLOTS, SLOTS, LANES), F32)]
    scratch += [pltpu.VMEM((SLOTS, LANES), F32)] * 2
    scratch += [pltpu.VMEM((n, 8, LANES), F32) for n in (NC, NZ, NX, NY)]
    scratch += [
        pltpu.VMEM((NZ * R, E), F32), pltpu.VMEM((NZ * R, E), F32), pltpu.VMEM((TILE, E), F32),
        pltpu.VMEM((NZ * R, E), BF16), pltpu.VMEM((4, R, E), BF16),
        pltpu.VMEM((2, R, E), BF16), pltpu.VMEM((2, HALF, E), BF16),
        pltpu.VMEM((3, TILE, E), BF16), pltpu.VMEM((3, TILE, E), BF16), pltpu.VMEM((TILE, E), F32),
        pltpu.VMEM((3, R, E), F32),
    ]
    for n in (24, 9, 15, 1, 7, 15, 1, 7, 3, 3, 2, 8, 12, 3):
        scratch += [dma((n,)), dma((n,))]
    return pl.pallas_call(
        kernel,
        out_shape=(
            jax.ShapeDtypeStruct((1,), F32),
            jax.ShapeDtypeStruct((R, E), F32),
            jax.ShapeDtypeStruct((R, E), F32),
        ),
        in_specs=[vmem, vmem, smem],
        out_specs=(smem, vmem, vmem),
        scratch_shapes=scratch,
        compiler_params=pltpu.CompilerParams(
            collective_id=0, has_side_effects=True, vmem_limit_bytes=56 * 2**20
        ),
    )(images, texts, logit_scale)


def solution(mesh):
    placed = (P(("row", "col"), None), P(("row", "col"), None), P())
    return jax.shard_map(
        local,
        mesh=mesh,
        in_specs=placed,
        out_specs=(P(), P(("row", "col"), None), P(("row", "col"), None)),
        check_vma=False,
    )
```

profile of v0, /device:TPU:1, one launch (start us, length us, event | category | flops | bytes accessed | tf_op | source)
XLA Modules:
  0.0 75.8 jit_solution(9989956335754055043)
XLA Ops:
  1.3 70.2 %shard_map.58 = (f32[1]{0:T(128)}, f32[96,768]{1,0:T(8,128)}, f32[96,768]{1,0:T(8,128)}) custom-call(bf16[96,768]{1,0:T(8,128)(2,1)} %images.1, bf16[96,768]{1,0:T(8,128)(2,1)} %texts.1, f32[1]{0:T(128)S(6)} %copy.9.scale_ref), custom_call_target="tpu_custom_call" | custom-call | tf_op jit(solution)/shard_map/pallas_call | solution.py:458
  72.2 0.0 copy-start
  72.2 1.7 %copy.11 = f32[96,768]{1,0:T(8,128)} copy(f32[96,768]{1,0:T(8,128)} %get-tuple-element.7) | data formatting | bytes 589824
  73.9 0.0 copy-done
  73.9 0.7 copy.12
Async XLA Ops:
  72.2 1.8 %copy-start = (f32[96,768]{1,0:T(8,128)S(1)}, f32[96,768]{1,0:T(8,128)}, u32[]{:S(2)}) copy-start(f32[96,768]{1,0:T(8,128)} %get-tuple-element.8) | copy-start | bytes 884740
where the time goes:
time: 75.9 us; the launch traced here: 75.8 us
  Pallas kernels  70.2 us (92%)
  between operations  3.1 us (4%)
  local copies, waits for them, and re-layouts  2.46 us (3%)
    pallas_call x1, Pallas kernels, local(): pl.pallas_call(kernel, out_shape=(jax.ShapeDtypeStruct((1,), F32), jax.Sh...  70.2 us
    unnamed x4, local copies, waits for them, and re-layouts  2.46 us

commit v1 on v0

--- a/solution.py
+++ b/solution.py
@@ -466,7 +466,7 @@
         out_specs=(smem, vmem, vmem),
         scratch_shapes=scratch,
         compiler_params=pltpu.CompilerParams(
-            collective_id=0, has_side_effects=True, vmem_limit_bytes=56 * 2**20
+            collective_id=0, has_side_effects=True, vmem_limit_bytes=44 * 2**20
         ),
     )(images, texts, logit_scale)
 

time: 75.9 us -> 75.3 us (level)
  Pallas kernels: 70.2 us -> 68.8 us
  local copies, waits for them, and re-layouts: 2.46 us -> 3.24 us
    pallas_call x1, Pallas kernels: 70.2 us -> 68.8 us  [local(): pl.pallas_call(kernel, out_shape=(jax.ShapeDtypeStruct((1,), F32), jax.Sh...]
    unnamed x4 -> x6, local copies, waits for them, and re-layouts: 2.46 us -> 3.24 us
where the time goes in v1:
time: 75.3 us; the launch traced here: 75.1 us
  Pallas kernels  68.8 us (91%)
  local copies, waits for them, and re-layouts  3.24 us (4%)
  between operations  3.05 us (4%)
    pallas_call x1, Pallas kernels, local(): pl.pallas_call(kernel, out_shape=(jax.ShapeDtypeStruct((1,), F32), jax.Sh...  68.8 us
    unnamed x6, local copies, waits for them, and re-layouts  3.24 us

profile of v1, /device:TPU:1, one launch (start us, length us, event | category | flops | bytes accessed | tf_op | source)
XLA Modules:
  0.0 75.1 jit_solution(9549382945475005599)
XLA Ops:
  1.3 0.0 copy-start
  1.3 0.9 %copy-done = bf16[96,768]{1,0:T(8,128)(2,1)S(1)} copy-done((bf16[96,768]{1,0:T(8,128)(2,1)S(1)}, bf16[96,768]{1,0:T(8,128)(2,1)}, u32[]{:S(2)}) %copy-start) | copy-done | bytes 147480
  2.2 0.0 copy-start.1
  2.2 0.9 %copy-done.1 = bf16[96,768]{1,0:T(8,128)(2,1)S(1)} copy-done((bf16[96,768]{1,0:T(8,128)(2,1)S(1)}, bf16[96,768]{1,0:T(8,128)(2,1)}, u32[]{:S(2)}) %copy-start.1) | copy-done | bytes 147480
  3.1 68.8 %shard_map.58 = (f32[1]{0:T(128)}, f32[96,768]{1,0:T(8,128)S(1)}, f32[96,768]{1,0:T(8,128)S(1)}) custom-call(bf16[96,768]{1,0:T(8,128)(2,1)S(1)} %copy-done, bf16[96,768]{1,0:T(8,128)(2,1)S(1)} %copy-done.1, f32[1]{0:T(128)S(6)} %copy.9.scale_ref), custom_call_target="tpu_custom_call" | custom-call | tf_op jit(solution)/shard_map/pallas_call | solution.py:458
  72.6 0.7 copy.11
  73.3 0.7 copy.12
Async XLA Ops:
  1.3 0.9 %copy-start = (bf16[96,768]{1,0:T(8,128)(2,1)S(1)}, bf16[96,768]{1,0:T(8,128)(2,1)}, u32[]{:S(2)}) copy-start(bf16[96,768]{1,0:T(8,128)(2,1)} %images.1) | copy-start | bytes 442372
  2.2 0.9 %copy-start.1 = (bf16[96,768]{1,0:T(8,128)(2,1)S(1)}, bf16[96,768]{1,0:T(8,128)(2,1)}, u32[]{:S(2)}) copy-start(bf16[96,768]{1,0:T(8,128)(2,1)} %texts.1) | copy-start | bytes 442372

commit v2 on v1

--- a/solution.py
+++ b/solution.py
@@ -376,9 +376,10 @@
 
     make_weights(12, 0, B, True)
     do_sib(1)
-    make_weights(4, 0, B, True)
+    make_weights(4, 3 * TILE, TILE, True)
     near_weights(3)
     do_q(3)
+    make_weights(4, 0, 3 * TILE)
     for cp in lx_cps + lc_cps:
         cp.wait_recv()
     ls_y[y] = total_of(ls_x, NX)

time: 75.3 us -> 75 us (level)
  no operation moved by 1% of the time
where the time goes in v2:
time: 75 us; the launch traced here: 74.8 us
  Pallas kernels  68.5 us (91%)
  local copies, waits for them, and re-layouts  3.24 us (4%)
  between operations  3.05 us (4%)
    pallas_call x1, Pallas kernels, local(): pl.pallas_call(kernel, out_shape=(jax.ShapeDtypeStruct((1,), F32), jax.Sh...  68.5 us
    unnamed x6, local copies, waits for them, and re-layouts  3.24 us

profile of v2, /device:TPU:1, one launch (start us, length us, event | category | flops | bytes accessed | tf_op | source)
XLA Modules:
  0.0 74.8 jit_solution(8682661374819120245)
XLA Ops:
  1.3 0.0 copy-start
  1.3 0.9 %copy-done = bf16[96,768]{1,0:T(8,128)(2,1)S(1)} copy-done((bf16[96,768]{1,0:T(8,128)(2,1)S(1)}, bf16[96,768]{1,0:T(8,128)(2,1)}, u32[]{:S(2)}) %copy-start) | copy-done | bytes 147480
  2.2 0.0 copy-start.1
  2.2 0.9 %copy-done.1 = bf16[96,768]{1,0:T(8,128)(2,1)S(1)} copy-done((bf16[96,768]{1,0:T(8,128)(2,1)S(1)}, bf16[96,768]{1,0:T(8,128)(2,1)}, u32[]{:S(2)}) %copy-start.1) | copy-done | bytes 147480
  3.1 68.5 %shard_map.58 = (f32[1]{0:T(128)}, f32[96,768]{1,0:T(8,128)S(1)}, f32[96,768]{1,0:T(8,128)S(1)}) custom-call(bf16[96,768]{1,0:T(8,128)(2,1)S(1)} %copy-done, bf16[96,768]{1,0:T(8,128)(2,1)S(1)} %copy-done.1, f32[1]{0:T(128)S(6)} %copy.9.scale_ref), custom_call_target="tpu_custom_call" | custom-call | tf_op jit(solution)/shard_map/pallas_call | solution.py:459
  72.3 0.7 copy.11
  73.0 0.7 copy.12
Async XLA Ops:
  1.3 0.9 %copy-start = (bf16[96,768]{1,0:T(8,128)(2,1)S(1)}, bf16[96,768]{1,0:T(8,128)(2,1)}, u32[]{:S(2)}) copy-start(bf16[96,768]{1,0:T(8,128)(2,1)} %images.1) | copy-start | bytes 442372
  2.2 0.9 %copy-start.1 = (bf16[96,768]{1,0:T(8,128)(2,1)S(1)}, bf16[96,768]{1,0:T(8,128)(2,1)}, u32[]{:S(2)}) copy-start(bf16[96,768]{1,0:T(8,128)(2,1)} %texts.1) | copy-start | bytes 442372
